TPU v7x, 32 devices: a whole 2x2x4 slice. The times are simulated.
32 devices in a mesh: dp: 4 (over y, x), expert: 8 (over z, core).
Axes of the slice: x: 2, y: 2, z: 4, core: 2. Of those that a mesh axis runs over, the one named last changes fastest.
Arguments:
- tokens: bfloat16 [4096, 2048], P(('dp', 'expert')), may hold values from -6 to 6
- expert_ids: int32 [4096, 2], P(('dp', 'expert')), may hold values from 0 to 7, as said below
- gate_values: float32 [4096, 2], P(('dp', 'expert')), may hold values from 0.05 to 0.5
- gate_up: bfloat16 [8, 2048, 1024], P('expert'), may hold values from -0.125 to 0.125
- down: bfloat16 [8, 512, 2048], P('expert'), may hold values from -0.25 to 0.25
- moment_first: bfloat16 [8, 512, 2048], P('expert'), may hold values from -6 to 6
- moment_second: bfloat16 [8, 512, 2048], P('expert'), may hold values from 1 to 100
- cotangent: bfloat16 [4096, 2048], P(('dp', 'expert')), may hold values from -6 to 6
Outputs:
- mixed: bfloat16 [4096, 2048], P(('dp', 'expert'))
- new_down: bfloat16 [8, 512, 2048], P('expert')
- new_first: bfloat16 [8, 512, 2048], P('expert')
- new_second: bfloat16 [8, 512, 2048], P('expert')
Inputs may be any that keep to these rules, and one draw needn't show every extreme that they name: `expert_ids`: each token names 2 different experts. In each data group one expert is named exactly 64 times by the tokens of every device of the group; every other expert is named at most 28 times by one device's tokens, and the other experts' counts on one device differ by one at most.
All inputs are finite; a program needn't handle non-finite values.
Results may differ from a plain program's by a relative error of at most 0.0058.
Values may be sent and summed in bfloat16 or wider, within the bound.
A program may use at most 128 MiB of HBM per device.

v0:
```python
import jax
import jax.numpy as jnp
from jax import lax
from jax.sharding import PartitionSpec as P

beta_one = 0.9
beta_two = 0.95
learn_rate = 0.01
decay_rate = 0.1
eps_value = 1e-08
first_fix = 1.0 - 0.9**10
second_fix = 1.0 - 0.95**10


def expert_apply(rows, gate_up_w, down_w, feature_half):
    projected = jnp.dot(rows, gate_up_w, preferred_element_type=jnp.float32)
    hidden_act = (jax.nn.silu(projected[:, :feature_half]) * projected[:, feature_half:]).astype(
        jnp.bfloat16
    )
    expert_out = jnp.dot(hidden_act, down_w, preferred_element_type=jnp.float32).astype(
        jnp.bfloat16
    )
    return (hidden_act, expert_out)


def adamw(gradient, down_w, first_old, second_old):
    first_new = beta_one * first_old.astype(jnp.float32) + (1.0 - beta_one) * gradient
    second_new = beta_two * second_old.astype(jnp.float32) + (1.0 - beta_two) * gradient * gradient
    step_size = first_new / first_fix / (jnp.sqrt(second_new / second_fix) + eps_value)
    down_new = down_w.astype(jnp.float32) * (1.0 - learn_rate * decay_rate) - learn_rate * step_size
    return (
        down_new.astype(jnp.bfloat16),
        first_new.astype(jnp.bfloat16),
        second_new.astype(jnp.bfloat16),
    )


def outer_sum(hidden_act, scaled_rows):
    return lax.dot_general(
        hidden_act, scaled_rows, (((0,), (0,)), ((), ())), preferred_element_type=jnp.float32
    )


def body(tokens, expert_ids, gate_values, gate_up, down, moment_first, moment_second, cotangent):
    tok_rows, feature_count = tokens.shape
    top_count = expert_ids.shape[1]
    hidden_count = down.shape[1]
    experts = lax.axis_size("expert")
    capacity = tok_rows // 2
    flat_ids = expert_ids.reshape(-1)
    assigns = flat_ids.shape[0]
    positions = jnp.arange(assigns, dtype=jnp.int32)
    onehot = (flat_ids[:, None] == jnp.arange(experts, dtype=jnp.int32)[None, :]).astype(jnp.int32)
    slot_rank = jnp.sum((jnp.cumsum(onehot, axis=0) - 1) * onehot, axis=1)
    scaled = (
        (gate_values[:, :, None] * cotangent[:, None, :].astype(jnp.float32))
        .astype(jnp.bfloat16)
        .reshape(assigns, feature_count)
    )
    zero_value = jnp.zeros((), jnp.bfloat16)
    send_mask = flat_ids >= 0
    bucket_rows = experts * capacity
    slot_index = flat_ids * capacity + slot_rank
    target = jnp.where(send_mask, slot_index, bucket_rows)
    slot_source = (
        jnp.full((bucket_rows,), assigns, jnp.int32).at[target].set(positions, mode="drop")
    )
    filled = slot_source < assigns
    safe = jnp.minimum(slot_source, assigns - 1)
    sent_rows = jnp.where(filled[:, None], tokens[safe // top_count], zero_value).reshape(
        experts, capacity, feature_count
    )
    sent_scaled = jnp.where(filled[:, None], scaled[safe], zero_value).reshape(
        experts, capacity, feature_count
    )
    recv_rows, recv_scaled = (
        lax.all_to_all(sent_rows, "expert", split_axis=0, concat_axis=0, tiled=True),
        lax.all_to_all(sent_scaled, "expert", split_axis=0, concat_axis=0, tiled=True),
    )
    hidden_act, expert_out = expert_apply(
        recv_rows.reshape(bucket_rows, feature_count), gate_up[0], down[0], hidden_count
    )
    gradient = outer_sum(hidden_act, recv_scaled.reshape(bucket_rows, feature_count))
    returned_rows = lax.all_to_all(
        expert_out.reshape(experts, capacity, feature_count),
        "expert",
        split_axis=0,
        concat_axis=0,
        tiled=True,
    )
    returned_rows = returned_rows.reshape(bucket_rows, feature_count)
    picked = returned_rows[jnp.where(send_mask, slot_index, 0)]
    weighted = gate_values[:, :, None] * picked.reshape(tok_rows, top_count, feature_count).astype(
        jnp.float32
    )
    mixed = jnp.sum(weighted, axis=1).astype(jnp.bfloat16)
    gradient = lax.psum(gradient, "dp")
    new_down, new_first, new_second = adamw(gradient, down[0], moment_first[0], moment_second[0])
    return (mixed, new_down[None], new_first[None], new_second[None])


def solution(mesh):
    return jax.shard_map(
        body,
        mesh=mesh,
        in_specs=(
            P(("dp", "expert"), None),
            P(("dp", "expert"), None),
            P(("dp", "expert"), None),
            P("expert", None, None),
            P("expert", None, None),
            P("expert", None, None),
            P("expert", None, None),
            P(("dp", "expert"), None),
        ),
        out_specs=(
            P(("dp", "expert"), None),
            P("expert", None, None),
            P("expert", None, None),
            P("expert", None, None),
        ),
        check_vma=False,
    )
```

profile of v0, /device:TPU:0, one launch (start us, length us, event | category | flops | bytes accessed | tf_op | source)
XLA Modules:
  0.0 260.2 jit_solution(14164256384085376664)
XLA Ops:
  7.2 0.7 broadcast_compare_fusion.1
  8.6 0.8 copy.16
  11.2 1.4 scatter_custom_fusion
  12.6 0.8 copy.13
  13.6 2.1 mul.116
  15.7 2.4 mul.117
  18.2 3.3 %gather_fusion = bf16[512,2048]{1,0:T(8,128)(2,1)} fusion(bf16[128,2048]{1,0:T(8,128)(2,1)S(1)} %copy-done, s32[1024]{0:T(1024)S(1)} %get-tuple-element.14), kind=kCustom, calls=%fused_computation | custom fusion | bytes 4196352 | tf_op jit(solution)/shard_map/gather | solution.py:70
  21.5 1.8 multiply_convert_fusion
  23.2 3.3 %gather_fusion.2 = bf16[512,2048]{1,0:T(8,128)(2,1)} fusion(bf16[256,2048]{1,0:T(8,128)(2,1)S(1)} %multiply_convert_fusion, s32[1024]{0:T(1024)S(1)} %get-tuple-element.13), kind=kCustom, calls=%fused_computation.2 | custom fusion | bytes 4196352 | tf_op jit(solution)/shard_map/gather | solution.py:73
  26.5 3.9 %broadcast_select_fusion = (bf16[8,64,2048]{2,1,0:T(8,128)(2,1)}, bf16[8,64,2048]{2,1,0:T(8,128)(2,1)S(1)}) fusion(bf16[8,64,2048]{2,1,0:T(8,128)(2,1)} %bitcast.57, pred[8,64]{1,0:T(8,128)(4,1)S(1)} %broadcast_in_dim.47, bf16[8,64,2048]{2,1,0:T(8,128)(2,1)} %bitcast.56), kind=kLoop, calls=%fused_computation.18 | loop fusion | flops 2097152 | bytes 8389120 | tf_op jit(solution)/shard_map/jit(_where)/select_n | solution.py:73
  30.4 55.3 %all_to_all.15 = bf16[8,64,2048]{2,1,0:T(8,128)(2,1)} all-to-all(bf16[8,64,2048]{2,1,0:T(8,128)(2,1)S(1)} %get-tuple-element.12), channel_id=1, replica_groups=mesh['dp'=4,'expert'=8] {'expert'}, dimensions={0} | all-to-all | bytes 4194304 | tf_op jit(solution)/shard_map/all_to_all | solution.py:77
  85.7 3.6 %all-to-all-start.2 = ((bf16[8,64,2048]{2,1,0:T(8,128)(2,1)}), bf16[8,64,2048]{2,1,0:T(8,128)(2,1)S(1)}, u32[]{:S(2)}, u32[]{:S(2)}) async-start(bf16[8,64,2048]{2,1,0:T(8,128)(2,1)} %get-tuple-element.11), calls=%async_computation.2 | async-start | bytes 4194304 | tf_op jit(solution)/shard_map/all_to_all | solution.py:78
  89.4 5.2 %fusion.1 = f32[512,1024]{1,0:T(8,128)S(1)} fusion(bf16[512,2048]{1,0:T(8,128)(2,1)} %bitcast.59, bf16[1,2048,1024]{2,1,0:T(8,128)(2,1)} %param.11), kind=kOutput, calls=%fused_computation.7 | convolution fusion | flops 2147483648 | bytes 8388608 | tf_op jit(solution)/shard_map/dot_general | solution.py:16
  94.8 43.5 %all-to-all-done.2 = bf16[8,64,2048]{2,1,0:T(8,128)(2,1)S(1)} async-done(((bf16[8,64,2048]{2,1,0:T(8,128)(2,1)}), bf16[8,64,2048]{2,1,0:T(8,128)(2,1)S(1)}, u32[]{:S(2)}, u32[]{:S(2)}) %all-to-all-start.2) | async-done | bytes 2097184 | tf_op jit(solution)/shard_map/all_to_all | solution.py:78
  138.3 3.2 %fusion.16 = f32[512,2048]{1,0:T(8,128)} fusion(bf16[512,512]{1,0:T(8,128)(2,1)S(1)} %fusion.9, bf16[512,2048]{1,0:T(8,128)(2,1)S(1)} %bitcast.58), kind=kOutput, calls=%fused_computation.48 | convolution fusion | flops 1073741824 | bytes 6815744 | tf_op jit(solution)/shard_map/dot_general | solution.py:39
  141.6 1.6 copy-done.1
  143.1 2.6 convolution_convert_fusion
  145.7 3.8 %all-to-all-start.1 = ((bf16[8,64,2048]{2,1,0:T(8,128)(2,1)}), bf16[8,64,2048]{2,1,0:T(8,128)(2,1)S(1)}, u32[]{:S(2)}, u32[]{:S(2)}) async-start(bf16[8,64,2048]{2,1,0:T(8,128)(2,1)} %bitcast.60), calls=%async_computation.1 | async-start | bytes 4194304 | tf_op jit(solution)/shard_map/all_to_all | solution.py:84
  149.5 48.8 %all-to-all-done.1 = bf16[8,64,2048]{2,1,0:T(8,128)(2,1)S(1)} async-done(((bf16[8,64,2048]{2,1,0:T(8,128)(2,1)}), bf16[8,64,2048]{2,1,0:T(8,128)(2,1)S(1)}, u32[]{:S(2)}, u32[]{:S(2)}) %all-to-all-start.1) | async-done | bytes 2097184 | tf_op jit(solution)/shard_map/all_to_all | solution.py:84
  198.3 2.3 gather_fusion.1
  200.6 2.4 reshape.139
  203.0 3.9 %multiply_reduce_fusion = bf16[128,2048]{1,0:T(8,128)(2,1)} fusion(f32[128,2,2048]{2,1,0:T(2,128)S(1)} %reshape.139, f32[128,2]{1,0:T(8,128)S(1)} %copy.13), kind=kLoop, calls=%fused_computation.17 | loop fusion | flops 786432 | bytes 2622464 | tf_op jit(solution)/shard_map/reduce_sum | solution.py:96
  207.0 37.5 %all-reduce.2.cloned.1.call-done = f32[512,2048]{1,0:T(8,128)} async-done(((f32[512,2048]{1,0:T(8,128)}), f32[512,2048]{1,0:T(8,128)}) %all-reduce.2.cloned.1.call-update) | async-done | bytes 4194320 | tf_op jit(solution)/shard_map/psum | solution.py:97
  244.5 8.9 %fusion.5 = (bf16[1,512,2048]{2,1,0:T(8,128)(2,1)}, bf16[1,512,2048]{2,1,0:T(8,128)(2,1)}, bf16[1,512,2048]{2,1,0:T(8,128)(2,1)}) fusion(f32[512,2048]{1,0:T(8,128)} %all-reduce.2.cloned.1.call-done, bf16[1,512,2048]{2,1,0:T(8,128)(2,1)} %param.14, bf16[1,512,2048]{2,1,0:T(8,128)(2,1)} %param.13, bf16[1,512,2048]{2,1,0:T(8,128)(2,1)} %param.12), kind=kLoop, calls=%fused_computation.13 | loop fusion | flops 20971520 | bytes 16777216 | tf_op jit(solution)/shard_map/broadcast_in_dim | solution.py:99
  (27 shorter events, 3.1 us)
Async XLA Ops:
  7.2 11.0 %copy-start = (bf16[128,2048]{1,0:T(8,128)(2,1)S(1)}, bf16[128,2048]{1,0:T(8,128)(2,1)}, u32[]{:S(2)}) copy-start(bf16[128,2048]{1,0:T(8,128)(2,1)} %param.8) | copy-start | bytes 1572868
  85.7 52.6 %all-to-all-start.2 = ((bf16[8,64,2048]{2,1,0:T(8,128)(2,1)}), bf16[8,64,2048]{2,1,0:T(8,128)(2,1)S(1)}, u32[]{:S(2)}, u32[]{:S(2)}) async-start(bf16[8,64,2048]{2,1,0:T(8,128)(2,1)} %get-tuple-element.11), calls=%async_computation.2 | async-start | bytes 4194304 | tf_op jit(solution)/shard_map/all_to_all | solution.py:78
  89.3 155.2 %all-reduce.2.cloned.1.call-start = ((), (), s32[]{:S(2)}) async-start(), calls=%async_computation.3 | async-start | bytes 8388608 | tf_op jit(solution)/shard_map/psum | solution.py:97
  141.5 1.6 copy-start.1
  145.7 52.6 %all-to-all-start.1 = ((bf16[8,64,2048]{2,1,0:T(8,128)(2,1)}), bf16[8,64,2048]{2,1,0:T(8,128)(2,1)S(1)}, u32[]{:S(2)}, u32[]{:S(2)}) async-start(bf16[8,64,2048]{2,1,0:T(8,128)(2,1)} %bitcast.60), calls=%async_computation.1 | async-start | bytes 4194304 | tf_op jit(solution)/shard_map/all_to_all | solution.py:84
Sparse Core Ops, SparseCore 0:
  141.7 102.7 all-reduce.1
where the time goes:
time: 261 us; the launch traced here: 260 us
  waiting for transfers between devices  130 us (50%)
  blocking collectives  55.3 us (21%)
  local copies, waits for them, and re-layouts  21.6 us (8%)
  other arithmetic  20.9 us (8%)
  between operations  14.2 us (5%)
  matrix products  11 us (4%)
  starting transfers between devices  7.43 us (3%)
    all_to_all x1, blocking collectives, body(): lax.all_to_all(sent_rows, 'expert', split_axis=0, concat_axis=0, tiled=True)  55.3 us
    all_to_all x1, waiting for transfers between devices, body(): lax.all_to_all(expert_out.reshape(experts, capacity, feature_count), 'exp...  48.8 us
    all_to_all x1, waiting for transfers between devices, body(): lax.all_to_all(sent_scaled, 'expert', split_axis=0, concat_axis=0, tiled=...  43.5 us
    psum x1, waiting for transfers between devices, body(): gradient = lax.psum(gradient, 'dp')  37.5 us
    broadcast_in_dim x1, other arithmetic, body(): return (mixed, new_down[None], new_first[None], new_second[None])  8.86 us
  transfers between devices with their start and end apart: 3, of which 3 were waited for; matrix products, arithmetic and copies ran while one was open for 6% of the time, Pallas kernels for 0%

commit v1 on v0

--- a/solution.py
+++ b/solution.py
@@ -1,6 +1,8 @@
 import jax
 import jax.numpy as jnp
 from jax import lax
+from jax.experimental import pallas as pl
+from jax.experimental.pallas import tpu as pltpu
 from jax.sharding import PartitionSpec as P
 
 beta_one = 0.9
@@ -99,9 +101,366 @@
     return (mixed, new_down[None], new_first[None], new_second[None])
 
 
+MESH = pl.DeviceIdType.MESH
+CHUNKS = 4
+SIDE = 4
+EXPERTS = 8
+
+
+def fused_kernel(
+    weights_ref, tokens_ref, cot_ref, gate_up_hbm, down_hbm, first_hbm, second_hbm,
+    mixed_ref, new_down_ref, new_first_ref, new_second_ref,
+    gate_up, down, first_old, second_old,
+    toks, cots, w_recv, w_cols, hidden, hidden_t, scaled, parts, peer_parts, from_left,
+    from_right, acc, grad, grad_send, grad_recv, grad_all, acc_grad,
+    load_sem, w_send, w_recv_sem, tok_send, tok_recv, cot_send, cot_recv,
+    part_send, part_recv, sum_send, left_recv, right_recv, gs_send, gs_recv, ga_send, ga_recv,
+):
+    expert = lax.axis_index("expert")
+    group = lax.axis_index("dp")
+    chip = expert // 2
+    core = expert % 2
+    other = 1 - core
+    rows, width = tokens_ref.shape
+    half = down.shape[0]
+    cw = width // CHUNKS
+    quarter = half // 4
+    group_x, group_y = group % 2, group // 2
+    peer = chip * 2 + other
+    right = jnp.minimum(chip + 1, SIDE - 1) * 2 + core
+    left = jnp.maximum(chip - 1, 0) * 2 + core
+
+    def dp_peer(k):
+        px = group_x if k == 2 else 1 - group_x
+        py = group_y if k == 1 else 1 - group_y
+        return py * 2 + px
+
+    def order(j):
+        near = chip + 1 - 2 * (chip % 2)
+        low = chip < 2
+        return (chip, near, jnp.where(low, 2, 1), jnp.where(low, 3, 0))[j]
+
+    def remote(src, dst, send, recv, target, axis="expert"):
+        return pltpu.make_async_remote_copy(
+            src_ref=src, dst_ref=dst, send_sem=send, recv_sem=recv,
+            device_id={axis: target}, device_id_type=MESH,
+        )
+
+    loads = [
+        pltpu.make_async_copy(src, dst, load_sem.at[i])
+        for i, (src, dst) in enumerate(
+            (
+                (gate_up_hbm.at[0], gate_up),
+                (down_hbm.at[0], down),
+                (first_hbm.at[0], first_old),
+                (second_hbm.at[0], second_old),
+            )
+        )
+    ]
+    for load in loads:
+        load.start()
+
+    barrier = pltpu.get_barrier_semaphore()
+    for k in range(1, EXPERTS):
+        pl.semaphore_signal(
+            barrier, inc=1, device_id={"expert": (expert + k) % EXPERTS}, device_id_type=MESH
+        )
+    for k in range(1, 4):
+        pl.semaphore_signal(barrier, inc=1, device_id={"dp": dp_peer(k)}, device_id_type=MESH)
+    toks[chip, core] = tokens_ref[...]
+    for n in range(CHUNKS):
+        cots[n, chip, core] = cot_ref[:, n * cw : (n + 1) * cw]
+    w_recv[expert] = weights_ref[expert]
+    pl.semaphore_wait(barrier, EXPERTS + 2)
+
+    def w_copy(k):
+        target = (expert + k) % EXPERTS
+        return remote(
+            weights_ref.at[target], w_recv.at[expert], w_send.at[k - 1], w_recv_sem.at[k - 1], target
+        )
+
+    def w_arrival(k):
+        source = (expert + EXPERTS - k) % EXPERTS
+        return remote(
+            weights_ref.at[source], w_recv.at[source], w_send.at[k - 1], w_recv_sem.at[k - 1], source
+        )
+
+    def gather_copies(buf, send, recv, j):
+        b = order(j)
+        block = buf.at[b, core]
+        return (
+            remote(block, block, send.at[j, 0], recv.at[b, core], right),
+            remote(block, block, send.at[j, 1], recv.at[b, core], left),
+            remote(block, block, send.at[j, 2], recv.at[b, core], peer),
+        )
+
+    def forward(buf, send, recv, j):
+        b = order(j)
+        to_right, to_left, to_peer = gather_copies(buf, send, recv, j)
+        if j > 0:
+            to_right.wait_recv()
+
+        @pl.when((b <= chip) & (chip < SIDE - 1))
+        def _():
+            to_right.start()
+
+        @pl.when((b >= chip) & (chip > 0))
+        def _():
+            to_left.start()
+
+        to_peer.start()
+
+    def from_peer(buf, send, recv, j):
+        b = order(j)
+        block = buf.at[b, other]
+        remote(block, block, send.at[j, 2], recv.at[b, other], peer).wait_recv()
+
+    def drain(buf, send, recv, j):
+        b = order(j)
+        to_right, to_left, to_peer = gather_copies(buf, send, recv, j)
+
+        @pl.when((b <= chip) & (chip < SIDE - 1))
+        def _():
+            to_right.wait_send()
+
+        @pl.when((b >= chip) & (chip > 0))
+        def _():
+            to_left.wait_send()
+
+        to_peer.wait_send()
+
+    tok_args = (toks, tok_send, tok_recv)
+
+    def cot_args(n):
+        return (cots.at[n], cot_send.at[n], cot_recv.at[n])
+
+    def part_copy(b):
+        return remote(
+            parts.at[b, other], peer_parts.at[b], part_send.at[b], part_recv.at[b], peer
+        )
+
+    def run_expert(j):
+        b = order(j)
+        tile = 256
+
+        @pl.loop(0, half // tile)
+        def _(n):
+            x = toks[b].reshape(2 * rows, width)
+            lo = pl.multiple_of(n * tile, tile)
+            hi = pl.multiple_of(half + n * tile, tile)
+            gate = jnp.dot(x, gate_up[:, pl.ds(lo, tile)], preferred_element_type=jnp.float32)
+            up = jnp.dot(x, gate_up[:, pl.ds(hi, tile)], preferred_element_type=jnp.float32)
+            act = gate / (1.0 + jnp.exp(-gate)) * up
+            hidden[:, pl.ds(lo, tile)] = act.astype(jnp.bfloat16)
+            at = pl.multiple_of(b * 2 * rows, 2 * rows)
+            hidden_t[pl.ds(lo, tile), pl.ds(at, 2 * rows)] = act.T.astype(jnp.bfloat16)
+
+        @pl.loop(0, width // 512)
+        def _(n):
+            at = pl.multiple_of(n * 512, 512)
+            out = jnp.dot(
+                hidden[...], down[:, pl.ds(at, 512)], preferred_element_type=jnp.float32
+            )
+            w = w_cols[b].reshape(2 * rows, 128)[:, 0:1]
+            parts[b, :, :, pl.ds(at, 512)] = (w * out).astype(jnp.bfloat16).reshape(2, rows, 512)
+
+        part_copy(b).start()
+
+    def sum_copies(b):
+        block = parts.at[b, core]
+        return (
+            remote(block, from_left.at[b], sum_send.at[b], left_recv.at[b], right),
+            remote(block, from_right.at[b], sum_send.at[b], right_recv.at[b], left),
+        )
+
+    def reduce_step(j):
+        b = order(j)
+        to_right, to_left = sum_copies(b)
+        part_copy(b).wait_recv()
+        acc[...] = parts[b, core].astype(jnp.float32) + peer_parts[b].astype(jnp.float32)
+
+        @pl.when((b >= chip) & (chip > 0))
+        def _():
+            to_right.wait_recv()
+            acc[...] += from_left[b].astype(jnp.float32)
+
+        @pl.when((b <= chip) & (chip < SIDE - 1))
+        def _():
+            to_left.wait_recv()
+            acc[...] += from_right[b].astype(jnp.float32)
+
+        if j == 0:
+            mixed_ref[...] = acc[...].astype(jnp.bfloat16)
+        else:
+            parts[b, core] = acc[...].astype(jnp.bfloat16)
+
+            @pl.when(b > chip)
+            def _():
+                to_right.start()
+
+            @pl.when(b < chip)
+            def _():
+                to_left.start()
+
+    def scatter_copy(n, k):
+        return remote(
+            grad_send.at[n, dp_peer(k)], grad_recv.at[n, k - 1], gs_send.at[n, k - 1],
+            gs_recv.at[n, k - 1], dp_peer(k), "dp",
+        )
+
+    def spread_copy(n, k, owner):
+        block = grad_all.at[n, owner]
+        return remote(
+            block, block, ga_send.at[n, k - 1], ga_recv.at[n, k - 1], dp_peer(k), "dp"
+        )
+
+    def gradient(n):
+        @pl.loop(0, SIDE)
+        def _(b):
+            w = w_cols[b].reshape(2 * rows, 128)[:, 0:1]
+            cot = cots[n, b].reshape(2 * rows, cw).astype(jnp.float32)
+            scaled[pl.ds(pl.multiple_of(b * 2 * rows, 2 * rows), 2 * rows), :] = (w * cot).astype(
+                jnp.bfloat16
+            )
+
+        @pl.loop(0, 2)
+        def _(m):
+            at = pl.multiple_of(m * 2 * quarter, 2 * quarter)
+            g = jnp.dot(
+                hidden_t[pl.ds(at, 2 * quarter), :], scaled[...], preferred_element_type=jnp.float32
+            )
+            g = g.reshape(2, quarter, cw)
+            grad[pl.ds(m * 2, 2)] = g
+            grad_send[n, pl.ds(m * 2, 2)] = g.astype(jnp.bfloat16)
+
+        for k in range(1, 4):
+            scatter_copy(n, k).start()
+        acc_grad[n] = grad[group]
+
+    def spread(n):
+        total = acc_grad[n]
+        for k in range(1, 4):
+            scatter_copy(n, k).wait_recv()
+            total = total + grad_recv[n, k - 1].astype(jnp.float32)
+        grad_all[n, group] = total.astype(jnp.bfloat16)
+        for k in range(1, 4):
+            spread_copy(n, k, group).start()
+
+    def update(n):
+        for k in range(1, 4):
+            spread_copy(n, k, dp_peer(k)).wait_recv()
+        columns = pl.ds(n * cw, cw)
+
+        @pl.loop(0, half // 32)
+        def _(i):
+            at = pl.ds(pl.multiple_of(i * 32, 32), 32)
+            per = quarter // 32
+            g = grad_all[n, i // per, pl.ds(pl.multiple_of((i % per) * 32, 32), 32), :]
+            new_down, new_first, new_second = adamw(
+                g.astype(jnp.float32), down[at, columns], first_old[at, columns],
+                second_old[at, columns],
+            )
+            new_down_ref[0, at, columns] = new_down
+            new_first_ref[0, at, columns] = new_first
+            new_second_ref[0, at, columns] = new_second
+
+    for k in range(1, EXPERTS):
+        w_copy(k).start()
+    forward(*tok_args, 0)
+    for k in range(1, EXPERTS):
+        w_arrival(k).wait_recv()
+    for s in range(EXPERTS):
+        w_cols[s // 2, s % 2] = jnp.broadcast_to(w_recv[s][0:1, :], (128, 128)).T
+    loads[0].wait()
+    loads[1].wait()
+    for j in range(SIDE):
+        if j > 0:
+            forward(*tok_args, j)
+        if j == 2:
+            forward(*cot_args(0), 0)
+        from_peer(*tok_args, j)
+        run_expert(j)
+    loads[2].wait()
+    loads[3].wait()
+    for n in range(CHUNKS):
+        forward(*cot_args(n), 1)
+        if n + 1 < CHUNKS:
+            forward(*cot_args(n + 1), 0)
+        forward(*cot_args(n), 2)
+        reduce_step(SIDE - 1 - n)
+        forward(*cot_args(n), 3)
+        for j in range(SIDE):
+            from_peer(*cot_args(n), j)
+        gradient(n)
+        if n >= 1:
+            spread(n - 1)
+        if n >= 2:
+            update(n - 2)
+    spread(CHUNKS - 1)
+    update(CHUNKS - 2)
+    update(CHUNKS - 1)
+    for j in range(SIDE):
+        drain(*tok_args, j)
+        for n in range(CHUNKS):
+            drain(*cot_args(n), j)
+        part_copy(order(j)).wait_send()
+        if j > 0:
+            sum_copies(order(j))[0].wait_send()
+    for k in range(1, EXPERTS):
+        w_copy(k).wait_send()
+    for n in range(CHUNKS):
+        for k in range(1, 4):
+            scatter_copy(n, k).wait_send()
+            spread_copy(n, k, group).wait_send()
+
+
+def fused_body(tokens, expert_ids, gate_values, gate_up, down, first, second, cotangent):
+    rows, width = tokens.shape
+    half = down.shape[1]
+    cw = width // CHUNKS
+    quarter = half // 4
+    chosen = expert_ids[None] == jnp.arange(EXPERTS, dtype=jnp.int32)[:, None, None]
+    weights = jnp.sum(jnp.where(chosen, gate_values[None], 0.0), axis=2)
+    weights = jnp.broadcast_to(weights[:, None, :], (EXPERTS, 8, rows))
+    bf, f32 = jnp.bfloat16, jnp.float32
+    vmem = pl.BlockSpec(memory_space=pltpu.VMEM)
+    hbm = pl.BlockSpec(memory_space=pl.ANY)
+    dma = pltpu.SemaphoreType.DMA
+    buffers = [
+        ((width, 2 * half), bf), ((half, width), bf), ((half, width), bf), ((half, width), bf),
+        ((SIDE, 2, rows, width), bf), ((CHUNKS, SIDE, 2, rows, cw), bf),
+        ((EXPERTS, 8, rows), f32), ((SIDE, 2, rows, 128), f32),
+        ((2 * rows, half), bf), ((half, EXPERTS * rows), bf), ((EXPERTS * rows, cw), bf),
+        ((SIDE, 2, rows, width), bf), ((SIDE, rows, width), bf), ((SIDE, rows, width), bf),
+        ((SIDE, rows, width), bf), ((rows, width), f32), ((4, quarter, cw), f32),
+        ((CHUNKS, 4, quarter, cw), bf), ((CHUNKS, 3, quarter, cw), bf),
+        ((CHUNKS, 4, quarter, cw), bf), ((CHUNKS, quarter, cw), f32),
+    ]
+    semaphores = [
+        (4,), (EXPERTS - 1,), (EXPERTS - 1,), (SIDE, 3), (SIDE, 2), (CHUNKS, SIDE, 3),
+        (CHUNKS, SIDE, 2), (SIDE,), (SIDE,), (SIDE,), (SIDE,), (SIDE,), (CHUNKS, 3), (CHUNKS, 3),
+        (CHUNKS, 3), (CHUNKS, 3),
+    ]
+    state = jax.ShapeDtypeStruct((1, half, width), bf)
+    return pl.pallas_call(
+        fused_kernel,
+        out_shape=(jax.ShapeDtypeStruct((rows, width), bf), state, state, state),
+        in_specs=[vmem, vmem, vmem, hbm, hbm, hbm, hbm],
+        out_specs=(vmem, vmem, vmem, vmem),
+        scratch_shapes=[pltpu.VMEM(s, t) for s, t in buffers] + [dma(s) for s in semaphores],
+        compiler_params=pltpu.CompilerParams(
+            collective_id=0, has_side_effects=True, vmem_limit_bytes=60 * 1024 * 1024
+        ),
+    )(weights, tokens, cotangent, gate_up, down, first, second)
+
+
 def solution(mesh):
+    def choose(*args):
+        fits = mesh.shape["expert"] == 8 and mesh.shape["dp"] == 4 and args[0].shape[0] == 128
+        return (fused_body if fits else body)(*args)
+
     return jax.shard_map(
-        body,
+        choose,
         mesh=mesh,
         in_specs=(
             P(("dp", "expert"), None),

time: 261 us -> 171 us (0.66)
  Pallas kernels: 0 us -> 160 us
  waiting for transfers between devices: 130 us -> 0 us
  blocking collectives: 55.3 us -> 0 us
  other arithmetic: 20.9 us -> 0.7 us
  between operations: 14.2 us -> 0.64 us
  local copies, waits for them, and re-layouts: 21.6 us -> 9.48 us
  matrix products: 11 us -> 0 us
  starting transfers between devices: 7.43 us -> 0 us
    pallas_call x0 -> x1, Pallas kernels: none -> 160 us  [fused_body(): pl.pallas_call(fused_kernel, out_shape=(jax.ShapeDtypeStruct((rows, width...]
    all_to_all x2 -> x0, waiting for transfers between devices: 92.2 us -> none  [the longest x1 48.8 us: body(): lax.all_to_all(expert_out.reshape(experts, capacity, feature_count), 'exp...]
    all_to_all x1 -> x0, blocking collectives: 55.3 us -> none  [body(): lax.all_to_all(sent_rows, 'expert', split_axis=0, concat_axis=0, tiled=True)]
    psum x1 -> x0, waiting for transfers between devices: 37.5 us -> none  [body(): gradient = lax.psum(gradient, 'dp')]
    dot_general x3 -> x0, matrix products: 11 us -> none  [the longest x1 5.15 us: expert_apply(): projected = jnp.dot(rows, gate_up_w, preferred_element_type=jnp.float32)]
    gather x3 -> x0, local copies, waits for them, and re-layouts: 8.89 us -> none  [the longest x1 3.28 us: body(): tokens[safe // top_count]]
    broadcast_in_dim x1 -> x0, other arithmetic: 8.86 us -> none  [body(): return (mixed, new_down[None], new_first[None], new_second[None])]
    all_to_all x2 -> x0, starting transfers between devices: 7.39 us -> none  [the longest x1 3.79 us: body(): lax.all_to_all(expert_out.reshape(experts, capacity, feature_count), 'exp...]
  transfers between devices with their start and end apart: 3 -> 0, of which waited for: 3 -> 0; matrix products, arithmetic and copies ran while one was open for 6% -> 0% of each run, Pallas kernels for 0% -> 0%
where the time goes in v1:
time: 171 us
  Pallas kernels  160 us (94%)
  local copies, waits for them, and re-layouts  9.48 us (6%)
    pallas_call x1, Pallas kernels, fused_body(): pl.pallas_call(fused_kernel, out_shape=(jax.ShapeDtypeStruct((rows, width...  160 us
    unnamed x8, local copies, waits for them, and re-layouts  8.86 us

profile of v1, /device:TPU:0, one launch (start us, length us, event | category | flops | bytes accessed | tf_op | source)
XLA Modules:
  0.0 171.1 jit_solution(15124386642705841318)
XLA Ops:
  0.6 0.7 select_reduce_fusion
  1.3 0.6 broadcast_in_dim.23.weights_ref
  2.0 160.3 %shard_map.111 = (bf16[128,2048]{1,0:T(8,128)(2,1)}, bf16[1,512,2048]{2,1,0:T(8,128)(2,1)}, bf16[1,512,2048]{2,1,0:T(8,128)(2,1)}, bf16[1,512,2048]{2,1,0:T(8,128)(2,1)}) custom-call(f32[8,8,128]{2,1,0:T(8,128)} %broadcast_in_dim.23.weights_ref, bf16[128,2048]{1,0:T(8,128)(2,1)} %tokens_ref.1, bf16[128,2048]{1,0:T(8,128)(2,1)} %cot_ref.1, ...), custom_call_target="tpu_custom_call" | custom-call | tf_op jit(solution)/shard_map/pallas_call | solution.py:445
  162.2 1.9 %copy.18 = bf16[128,2048]{1,0:T(8,128)(2,1)} copy(bf16[128,2048]{1,0:T(8,128)(2,1)} %get-tuple-element.8) | data formatting | bytes 1048576
  164.1 0.0 copy-start.1
  164.1 3.3 %copy.19 = bf16[1,512,2048]{2,1,0:T(8,128)(2,1)} copy(bf16[1,512,2048]{2,1,0:T(8,128)(2,1)} %get-tuple-element.9) | data formatting | bytes 4194304
  167.4 0.0 copy-done.1
  167.4 0.0 copy-start
  167.4 1.3 copy.20
  168.7 1.0 copy-done
  169.8 1.3 copy.21
Async XLA Ops:
  164.1 3.3 %copy-start.1 = (bf16[1,512,2048]{2,1,0:T(8,128)(2,1)S(1)}, bf16[1,512,2048]{2,1,0:T(8,128)(2,1)}, u32[]{:S(2)}) copy-start(bf16[1,512,2048]{2,1,0:T(8,128)(2,1)} %get-tuple-element.10) | copy-start | bytes 6291460
  167.4 2.3 %copy-start = (bf16[1,512,2048]{2,1,0:T(8,128)(2,1)S(1)}, bf16[1,512,2048]{2,1,0:T(8,128)(2,1)}, u32[]{:S(2)}) copy-start(bf16[1,512,2048]{2,1,0:T(8,128)(2,1)} %get-tuple-element.11) | copy-start | bytes 6291460

commit v2 on v1

--- a/solution.py
+++ b/solution.py
@@ -103,14 +103,13 @@
 
 MESH = pl.DeviceIdType.MESH
 CHUNKS = 4
+PIECES = 2
 SIDE = 4
 EXPERTS = 8
 
 
 def fused_kernel(
-    weights_ref, tokens_ref, cot_ref, gate_up_hbm, down_hbm, first_hbm, second_hbm,
-    mixed_ref, new_down_ref, new_first_ref, new_second_ref,
-    gate_up, down, first_old, second_old,
+    weights_ref, tokens_ref, cot_ref, gate_up_hbm, down_hbm, mixed_ref, grad_ref, gate_up, down,
     toks, cots, w_recv, w_cols, hidden, hidden_t, scaled, parts, peer_parts, from_left,
     from_right, acc, grad, grad_send, grad_recv, grad_all, acc_grad,
     load_sem, w_send, w_recv_sem, tok_send, tok_recv, cot_send, cot_recv,
@@ -152,8 +151,6 @@
             (
                 (gate_up_hbm.at[0], gate_up),
                 (down_hbm.at[0], down),
-                (first_hbm.at[0], first_old),
-                (second_hbm.at[0], second_old),
             )
         )
     ]
@@ -185,18 +182,18 @@
             weights_ref.at[source], w_recv.at[source], w_send.at[k - 1], w_recv_sem.at[k - 1], source
         )
 
-    def gather_copies(buf, send, recv, j):
+    def gather_copies(view, send, recv, j):
         b = order(j)
-        block = buf.at[b, core]
+        block = view(b, core)
         return (
             remote(block, block, send.at[j, 0], recv.at[b, core], right),
             remote(block, block, send.at[j, 1], recv.at[b, core], left),
             remote(block, block, send.at[j, 2], recv.at[b, core], peer),
         )
 
-    def forward(buf, send, recv, j):
+    def forward(view, send, recv, j):
         b = order(j)
-        to_right, to_left, to_peer = gather_copies(buf, send, recv, j)
+        to_right, to_left, to_peer = gather_copies(view, send, recv, j)
         if j > 0:
             to_right.wait_recv()
 
@@ -210,14 +207,14 @@
 
         to_peer.start()
 
-    def from_peer(buf, send, recv, j):
+    def from_peer(view, send, recv, j):
         b = order(j)
-        block = buf.at[b, other]
+        block = view(b, other)
         remote(block, block, send.at[j, 2], recv.at[b, other], peer).wait_recv()
 
-    def drain(buf, send, recv, j):
+    def drain(view, send, recv, j):
         b = order(j)
-        to_right, to_left, to_peer = gather_copies(buf, send, recv, j)
+        to_right, to_left, to_peer = gather_copies(view, send, recv, j)
 
         @pl.when((b <= chip) & (chip < SIDE - 1))
         def _():
@@ -229,10 +226,15 @@
 
         to_peer.wait_send()
 
-    tok_args = (toks, tok_send, tok_recv)
+    piece = rows // PIECES
+
+    def tok_args(h):
+        return (
+            lambda b, c: toks.at[b, c, pl.ds(h * piece, piece)], tok_send.at[h], tok_recv.at[h]
+        )
 
     def cot_args(n):
-        return (cots.at[n], cot_send.at[n], cot_recv.at[n])
+        return (lambda b, c: cots.at[n, b, c], cot_send.at[n], cot_recv.at[n])
 
     def part_copy(b):
         return remote(
@@ -346,61 +348,76 @@
         for k in range(1, 4):
             spread_copy(n, k, group).start()
 
-    def update(n):
+    def collect(n):
         for k in range(1, 4):
             spread_copy(n, k, dp_peer(k)).wait_recv()
-        columns = pl.ds(n * cw, cw)
-
-        @pl.loop(0, half // 32)
-        def _(i):
-            at = pl.ds(pl.multiple_of(i * 32, 32), 32)
-            per = quarter // 32
-            g = grad_all[n, i // per, pl.ds(pl.multiple_of((i % per) * 32, 32), 32), :]
-            new_down, new_first, new_second = adamw(
-                g.astype(jnp.float32), down[at, columns], first_old[at, columns],
-                second_old[at, columns],
-            )
-            new_down_ref[0, at, columns] = new_down
-            new_first_ref[0, at, columns] = new_first
-            new_second_ref[0, at, columns] = new_second
+        for q in range(4):
+            grad_ref[q * quarter : (q + 1) * quarter, n * cw : (n + 1) * cw] = grad_all[n, q]
+
+    is_end = (chip == 0) | (chip == SIDE - 1)
+
+    def end_reduce(j):
+        pl.when(is_end)(lambda: reduce_step(j))
+
+    def middle_reduce(j):
+        pl.when(jnp.logical_not(is_end))(lambda: reduce_step(j))
 
     for k in range(1, EXPERTS):
         w_copy(k).start()
-    forward(*tok_args, 0)
+    for h in range(PIECES):
+        forward(*tok_args(h), 0)
     for k in range(1, EXPERTS):
         w_arrival(k).wait_recv()
     for s in range(EXPERTS):
         w_cols[s // 2, s % 2] = jnp.broadcast_to(w_recv[s][0:1, :], (128, 128)).T
-    loads[0].wait()
-    loads[1].wait()
+    for load in loads:
+        load.wait()
+    def pass_on(j):
+        for h in range(PIECES):
+            forward(*tok_args(h), j)
+
+    is_middle = jnp.logical_not(is_end)
     for j in range(SIDE):
-        if j > 0:
-            forward(*tok_args, j)
+        if j == 1:
+            pass_on(1)
+        if j >= 2:
+            pl.when(is_end)(lambda: pass_on(j))
+        if 1 <= j < SIDE - 1:
+            pl.when(is_middle)(lambda: pass_on(j + 1))
         if j == 2:
             forward(*cot_args(0), 0)
-        from_peer(*tok_args, j)
+            forward(*cot_args(1), 0)
+        if j >= 2:
+            end_reduce(j - 1)
+        for h in range(PIECES):
+            from_peer(*tok_args(h), j)
         run_expert(j)
-    loads[2].wait()
-    loads[3].wait()
+    forward(*cot_args(0), 1)
+    forward(*cot_args(0), 2)
+    end_reduce(SIDE - 1)
     for n in range(CHUNKS):
-        forward(*cot_args(n), 1)
+        if n + 2 < CHUNKS:
+            forward(*cot_args(n + 2), 0)
+        forward(*cot_args(n), 3)
         if n + 1 < CHUNKS:
-            forward(*cot_args(n + 1), 0)
-        forward(*cot_args(n), 2)
-        reduce_step(SIDE - 1 - n)
-        forward(*cot_args(n), 3)
+            forward(*cot_args(n + 1), 1)
+            forward(*cot_args(n + 1), 2)
+        if n >= 1:
+            middle_reduce((2, 3, 1)[n - 1])
         for j in range(SIDE):
             from_peer(*cot_args(n), j)
         gradient(n)
         if n >= 1:
             spread(n - 1)
         if n >= 2:
-            update(n - 2)
+            collect(n - 2)
+    reduce_step(0)
     spread(CHUNKS - 1)
-    update(CHUNKS - 2)
-    update(CHUNKS - 1)
+    collect(CHUNKS - 2)
+    collect(CHUNKS - 1)
     for j in range(SIDE):
-        drain(*tok_args, j)
+        for h in range(PIECES):
+            drain(*tok_args(h), j)
         for n in range(CHUNKS):
             drain(*cot_args(n), j)
         part_copy(order(j)).wait_send()
@@ -427,7 +444,7 @@
     hbm = pl.BlockSpec(memory_space=pl.ANY)
     dma = pltpu.SemaphoreType.DMA
     buffers = [
-        ((width, 2 * half), bf), ((half, width), bf), ((half, width), bf), ((half, width), bf),
+        ((width, 2 * half), bf), ((half, width), bf),
         ((SIDE, 2, rows, width), bf), ((CHUNKS, SIDE, 2, rows, cw), bf),
         ((EXPERTS, 8, rows), f32), ((SIDE, 2, rows, 128), f32),
         ((2 * rows, half), bf), ((half, EXPERTS * rows), bf), ((EXPERTS * rows, cw), bf),
@@ -437,21 +454,24 @@
         ((CHUNKS, 4, quarter, cw), bf), ((CHUNKS, quarter, cw), f32),
     ]
     semaphores = [
-        (4,), (EXPERTS - 1,), (EXPERTS - 1,), (SIDE, 3), (SIDE, 2), (CHUNKS, SIDE, 3),
+        (2,), (EXPERTS - 1,), (EXPERTS - 1,), (PIECES, SIDE, 3), (PIECES, SIDE, 2), (CHUNKS, SIDE, 3),
         (CHUNKS, SIDE, 2), (SIDE,), (SIDE,), (SIDE,), (SIDE,), (SIDE,), (CHUNKS, 3), (CHUNKS, 3),
         (CHUNKS, 3), (CHUNKS, 3),
     ]
-    state = jax.ShapeDtypeStruct((1, half, width), bf)
-    return pl.pallas_call(
+    mixed, gradient = pl.pallas_call(
         fused_kernel,
-        out_shape=(jax.ShapeDtypeStruct((rows, width), bf), state, state, state),
-        in_specs=[vmem, vmem, vmem, hbm, hbm, hbm, hbm],
-        out_specs=(vmem, vmem, vmem, vmem),
+        out_shape=(
+            jax.ShapeDtypeStruct((rows, width), bf), jax.ShapeDtypeStruct((half, width), bf)
+        ),
+        in_specs=[vmem, vmem, vmem, hbm, hbm],
+        out_specs=(vmem, vmem),
         scratch_shapes=[pltpu.VMEM(s, t) for s, t in buffers] + [dma(s) for s in semaphores],
         compiler_params=pltpu.CompilerParams(
-            collective_id=0, has_side_effects=True, vmem_limit_bytes=60 * 1024 * 1024
+            collective_id=0, has_side_effects=True, vmem_limit_bytes=56 * 1024 * 1024
         ),
-    )(weights, tokens, cotangent, gate_up, down, first, second)
+    )(weights, tokens, cotangent, gate_up, down)
+    states = adamw(gradient[None].astype(f32), down, first, second)
+    return (mixed, *states)
 
 
 def solution(mesh):

time: 171 us -> 136 us (0.80)
  Pallas kernels: 160 us -> 125 us
  local copies, waits for them, and re-layouts: 9.48 us -> 1.43 us
  other arithmetic: 0.7 us -> 8.5 us
    pallas_call x1, Pallas kernels: 160 us -> 125 us  [fused_body(): pl.pallas_call(fused_kernel, out_shape=(jax.ShapeDtypeStruct((rows, width...]
    unnamed x8 -> x9, local copies, waits for them, and re-layouts: 8.86 us -> 0.81 us
    convert_element_type x0 -> x1, other arithmetic: none -> 7.64 us  [adamw(): second_new.astype(jnp.bfloat16)]
where the time goes in v2:
time: 136 us
  Pallas kernels  125 us (92%)
  other arithmetic  8.5 us (6%)
  local copies, waits for them, and re-layouts  1.43 us (1%)
    pallas_call x1, Pallas kernels, fused_body(): pl.pallas_call(fused_kernel, out_shape=(jax.ShapeDtypeStruct((rows, width...  125 us
    convert_element_type x1, other arithmetic, adamw(): second_new.astype(jnp.bfloat16)  7.64 us

profile of v2, /device:TPU:0, one launch (start us, length us, event | category | flops | bytes accessed | tf_op | source)
XLA Modules:
  0.0 135.8 jit_solution(17450903877554132340)
XLA Ops:
  0.6 0.0 copy-start
  0.6 0.0 copy-start.1
  0.7 0.0 copy-start.2
  0.7 0.9 select_reduce_fusion
  1.5 0.6 broadcast_in_dim.24.weights_ref
  2.1 125.2 %shard_map.111 = (bf16[128,2048]{1,0:T(8,128)(2,1)}, bf16[512,2048]{1,0:T(8,128)(2,1)}) custom-call(f32[8,8,128]{2,1,0:T(8,128)} %broadcast_in_dim.24.weights_ref, bf16[128,2048]{1,0:T(8,128)(2,1)} %tokens_ref.1, bf16[128,2048]{1,0:T(8,128)(2,1)} %cot_ref.1, bf16[1,2048,1024]{2,1,0:T(8,128)(2,1)} %gate_up_hbm.1, bf16[1,512,2048]{2,1,0:T(8,128)(2,1)} %down_hbm.1), custom_call_target="tpu_custom_call" | custom-call | tf_op jit(solution)/shard_map/pallas_call | solution.py:461
  127.3 0.0 copy-done
  127.3 0.0 copy-done.1
  127.3 0.0 copy-done.2
  127.3 0.0 copy-start.3
  127.3 7.6 %fusion.4 = (bf16[1,512,2048]{2,1,0:T(8,128)(2,1)}, bf16[1,512,2048]{2,1,0:T(8,128)(2,1)}, bf16[1,512,2048]{2,1,0:T(8,128)(2,1)}) fusion(bf16[512,2048]{1,0:T(8,128)(2,1)} %get-tuple-element.7, bf16[1,512,2048]{2,1,0:T(8,128)(2,1)S(1)} %copy-done.1, bf16[1,512,2048]{2,1,0:T(8,128)(2,1)S(1)} %copy-done.2, bf16[1,512,2048]{2,1,0:T(8,128)(2,1)S(1)} %copy-done), kind=kLoop, calls=%fused_computation.7 | loop fusion | flops 22020096 | bytes 14680064 | tf_op jit(solution)/shard_map/convert_element_type | solution.py:36
  135.0 0.0 copy-done.3
  135.0 0.8 copy.15
Async XLA Ops:
  0.6 126.7 %copy-start = (bf16[1,512,2048]{2,1,0:T(8,128)(2,1)S(1)}, bf16[1,512,2048]{2,1,0:T(8,128)(2,1)}, u32[]{:S(2)}) copy-start(bf16[1,512,2048]{2,1,0:T(8,128)(2,1)} %down_hbm.1) | copy-start | bytes 6291460
  0.6 126.7 %copy-start.1 = (bf16[1,512,2048]{2,1,0:T(8,128)(2,1)S(1)}, bf16[1,512,2048]{2,1,0:T(8,128)(2,1)}, u32[]{:S(2)}) copy-start(bf16[1,512,2048]{2,1,0:T(8,128)(2,1)} %param.14) | copy-start | bytes 6291460
  0.7 126.7 %copy-start.2 = (bf16[1,512,2048]{2,1,0:T(8,128)(2,1)S(1)}, bf16[1,512,2048]{2,1,0:T(8,128)(2,1)}, u32[]{:S(2)}) copy-start(bf16[1,512,2048]{2,1,0:T(8,128)(2,1)} %param.13) | copy-start | bytes 6291460
  127.3 7.7 %copy-start.3 = (bf16[128,2048]{1,0:T(8,128)(2,1)S(1)}, bf16[128,2048]{1,0:T(8,128)(2,1)}, u32[]{:S(2)}) copy-start(bf16[128,2048]{1,0:T(8,128)(2,1)} %get-tuple-element.15) | copy-start | bytes 1572868

commit v3 on v2

--- a/solution.py
+++ b/solution.py
@@ -28,8 +28,9 @@
 def adamw(gradient, down_w, first_old, second_old):
     first_new = beta_one * first_old.astype(jnp.float32) + (1.0 - beta_one) * gradient
     second_new = beta_two * second_old.astype(jnp.float32) + (1.0 - beta_two) * gradient * gradient
-    step_size = first_new / first_fix / (jnp.sqrt(second_new / second_fix) + eps_value)
-    down_new = down_w.astype(jnp.float32) * (1.0 - learn_rate * decay_rate) - learn_rate * step_size
+    second_hat = second_new * (1.0 / second_fix)
+    step_size = first_new * (learn_rate / first_fix) / (second_hat * lax.rsqrt(second_hat) + eps_value)
+    down_new = down_w.astype(jnp.float32) * (1.0 - learn_rate * decay_rate) - step_size
     return (
         down_new.astype(jnp.bfloat16),
         first_new.astype(jnp.bfloat16),
@@ -387,6 +388,7 @@
         if j == 2:
             forward(*cot_args(0), 0)
             forward(*cot_args(1), 0)
+            forward(*cot_args(2), 0)
         if j >= 2:
             end_reduce(j - 1)
         for h in range(PIECES):
@@ -396,8 +398,8 @@
     forward(*cot_args(0), 2)
     end_reduce(SIDE - 1)
     for n in range(CHUNKS):
-        if n + 2 < CHUNKS:
-            forward(*cot_args(n + 2), 0)
+        if n + 3 < CHUNKS:
+            forward(*cot_args(n + 3), 0)
         forward(*cot_args(n), 3)
         if n + 1 < CHUNKS:
             forward(*cot_args(n + 1), 1)

time: 136 us -> 127 us (0.934)
  Pallas kernels: 125 us -> 117 us
    pallas_call x1, Pallas kernels: 125 us -> 117 us  [fused_body(): pl.pallas_call(fused_kernel, out_shape=(jax.ShapeDtypeStruct((rows, width...]
where the time goes in v3:
time: 127 us
  Pallas kernels  117 us (92%)
  other arithmetic  7.76 us (6%)
  local copies, waits for them, and re-layouts  1.43 us (1%)
    pallas_call x1, Pallas kernels, fused_body(): pl.pallas_call(fused_kernel, out_shape=(jax.ShapeDtypeStruct((rows, width...  117 us
    convert_element_type x1, other arithmetic, adamw(): second_new.astype(jnp.bfloat16)  6.9 us

profile of v3, /device:TPU:0, one launch (start us, length us, event | category | flops | bytes accessed | tf_op | source)
XLA Modules:
  0.0 126.8 jit_solution(16431103992792953173)
XLA Ops:
  0.6 0.0 copy-start
  0.6 0.0 copy-start.1
  0.7 0.0 copy-start.2
  0.7 0.9 select_reduce_fusion
  1.5 0.6 broadcast_in_dim.24.weights_ref
  2.1 117.0 %shard_map.111 = (bf16[128,2048]{1,0:T(8,128)(2,1)}, bf16[512,2048]{1,0:T(8,128)(2,1)}) custom-call(f32[8,8,128]{2,1,0:T(8,128)} %broadcast_in_dim.24.weights_ref, bf16[128,2048]{1,0:T(8,128)(2,1)} %tokens_ref.1, bf16[128,2048]{1,0:T(8,128)(2,1)} %cot_ref.1, bf16[1,2048,1024]{2,1,0:T(8,128)(2,1)} %gate_up_hbm.1, bf16[1,512,2048]{2,1,0:T(8,128)(2,1)} %down_hbm.1), custom_call_target="tpu_custom_call" | custom-call | tf_op jit(solution)/shard_map/pallas_call | solution.py:463
  119.1 0.0 copy-done
  119.1 0.0 copy-done.1
  119.1 0.0 copy-done.2
  119.1 0.0 copy-start.3
  119.1 6.9 %fusion.8 = (bf16[1,512,2048]{2,1,0:T(8,128)(2,1)}, bf16[1,512,2048]{2,1,0:T(8,128)(2,1)}, bf16[1,512,2048]{2,1,0:T(8,128)(2,1)}) fusion(bf16[512,2048]{1,0:T(8,128)(2,1)} %get-tuple-element.7, bf16[1,512,2048]{2,1,0:T(8,128)(2,1)S(1)} %copy-done.1, bf16[1,512,2048]{2,1,0:T(8,128)(2,1)S(1)} %copy-done.2, bf16[1,512,2048]{2,1,0:T(8,128)(2,1)S(1)} %copy-done), kind=kLoop, calls=%fused_computation.11 | loop fusion | flops 22020096 | bytes 14680064 | tf_op jit(solution)/shard_map/convert_element_type | solution.py:37
  126.0 0.0 copy-done.3
  126.0 0.8 copy.15
Async XLA Ops:
  0.6 118.5 %copy-start = (bf16[1,512,2048]{2,1,0:T(8,128)(2,1)S(1)}, bf16[1,512,2048]{2,1,0:T(8,128)(2,1)}, u32[]{:S(2)}) copy-start(bf16[1,512,2048]{2,1,0:T(8,128)(2,1)} %down_hbm.1) | copy-start | bytes 6291460
  0.6 118.5 %copy-start.1 = (bf16[1,512,2048]{2,1,0:T(8,128)(2,1)S(1)}, bf16[1,512,2048]{2,1,0:T(8,128)(2,1)}, u32[]{:S(2)}) copy-start(bf16[1,512,2048]{2,1,0:T(8,128)(2,1)} %param.14) | copy-start | bytes 6291460
  0.7 118.5 %copy-start.2 = (bf16[1,512,2048]{2,1,0:T(8,128)(2,1)S(1)}, bf16[1,512,2048]{2,1,0:T(8,128)(2,1)}, u32[]{:S(2)}) copy-start(bf16[1,512,2048]{2,1,0:T(8,128)(2,1)} %param.13) | copy-start | bytes 6291460
  119.1 6.9 %copy-start.3 = (bf16[128,2048]{1,0:T(8,128)(2,1)S(1)}, bf16[128,2048]{1,0:T(8,128)(2,1)}, u32[]{:S(2)}) copy-start(bf16[128,2048]{1,0:T(8,128)(2,1)} %get-tuple-element.15) | copy-start | bytes 1572868
